TPU v7x, 32 devices: a whole 2x2x4 slice. The times are simulated.
32 devices in a mesh: dp: 2 (over x), space: 16 (over z, y, core).
Axes of the slice: x: 2, y: 2, z: 4, core: 2. Of those that a mesh axis runs over, the one named last changes fastest.
Arguments:
- activations: bfloat16 [4, 16, 64, 256], P('dp', 'space'), may hold values from -6 to 6
- out_grads: bfloat16 [4, 16, 64, 256], P('dp', 'space'), may hold values from -6 to 6
- old_input_factor: bfloat16 [2304, 2304], P(('dp', 'space')), may hold values from -3 to 3
- old_grad_factor: float32 [256, 256], P('space'), may hold values from -3 to 3
Outputs:
- input_factor: float32 [2304, 2304], P(('dp', 'space'))
- grad_factor: float32 [256, 256], P('space')
All inputs are finite; a program needn't handle non-finite values.
Results may differ from a plain program's by a relative error of at most 0.00055.
Values may be sent and summed in bfloat16 or wider, within the bound.
A program may use at most 128 MiB of HBM per device.

v0:
```python
import jax
import jax.numpy as jnp
from jax import lax
from jax.experimental import pallas as pl
from jax.experimental.pallas import tpu as pltpu
from jax.sharding import PartitionSpec as P


def extended(block, sides, width):
    for axis, dim in sides:
        count = lax.axis_size(axis)
        forward = [(i, i + 1) for i in range(count - 1)]
        backward = [(target, source) for source, target in forward]
        low = lax.ppermute(
            lax.slice_in_dim(block, block.shape[dim] - width, None, axis=dim), axis, forward
        )
        high = lax.ppermute(lax.slice_in_dim(block, 0, width, axis=dim), axis, backward)
        block = jnp.concatenate([low, block, high], axis=dim)
    return block


def transposed_product(left, right):
    return lax.dot_general(
        left, right, (((0,), (0,)), ((), ())), preferred_element_type=jnp.float32
    )


def reduced_form(activations, out_grads, old_input_factor, old_grad_factor):
    images, rows_here, columns_here, channels = activations.shape
    widened = extended(activations, (("space", 1),), 1)
    padded = jnp.pad(widened, ((0, 0), (0, 0), (1, 1), (0, 0)))
    pieces = [
        padded[:, ky : ky + rows_here, kx : kx + columns_here, :]
        for ky in range(3)
        for kx in range(3)
    ]
    patches = jnp.concatenate(pieces, axis=3).reshape(
        images * rows_here * columns_here, 9 * channels
    )
    groups = lax.axis_size("dp")
    spaces = lax.axis_size("space")
    positions = images * groups * rows_here * spaces * columns_here
    share = old_input_factor.shape[0]
    width_all = patches.shape[1]
    column_blocks = 4
    block_width = width_all // column_blocks
    results = []
    block = share * groups
    for which in range(column_blocks):
        right = patches[:, which * block_width : (which + 1) * block_width]

        def mapped_block(start, count, right=right):
            offsets = jnp.arange(count, dtype=jnp.int32)
            holder_space = offsets // block
            within_block = offsets % block
            holder_group = within_block // share
            within = within_block % share
            columns = holder_group * (spaces * share) + holder_space * share + within
            left = jnp.take(patches, columns, axis=1)
            return transposed_product(left, right)

        results.append(
            lax.psum_scatter(
                mapped_block(jnp.int32(0), block * lax.axis_size("space")),
                "space",
                scatter_dimension=0,
                tiled=True,
            )
        )
    part_sum = jnp.concatenate(results, axis=1)
    input_sum = lax.psum_scatter(
        part_sum.astype(jnp.bfloat16), "dp", scatter_dimension=0, tiled=True
    ).astype(jnp.float32)
    flat_grads = out_grads.reshape(images * rows_here * columns_here, channels)
    grad_term = transposed_product(flat_grads, flat_grads)
    grad_rows_here = old_grad_factor.shape[0]
    grad_total = lax.psum(grad_term, ("dp", "space"))
    grad_sum = lax.dynamic_slice_in_dim(
        grad_total, lax.axis_index("space") * grad_rows_here, grad_rows_here, 0
    )
    input_factor = 0.5 * old_input_factor.astype(jnp.float32) + 0.5 / positions * input_sum
    grad_factor = 0.5 * old_grad_factor + 0.5 / positions * grad_sum
    return (input_factor, grad_factor)


MESH = pl.DeviceIdType.MESH
TAPS = 3


def gather_kernel(act, grad, sums, grad_sum, maps, acc, gbuf, gpart, grecv,
                  sz, rz, sx, rx, sy, ry, sdx, rdx, sdy, rdy, sp, rp, sg, rg, ss, rs):
    images, rows, columns, channels = act.shape
    share = sums.shape[0]
    height = maps.shape[1] - 2
    spaces = height // rows
    lines = spaces // 4
    x = lax.axis_index("dp")
    space = lax.axis_index("space")
    core = space % 2
    y = (space // 2) % 2
    z = space // 4
    half = z // 2
    order = [z, z + 1 - 2 * (z % 2), 2 - half, 3 - 3 * half]
    x_other, y_other = 1 - x, 1 - y

    def place(line, yy, kk):
        return line * 4 + yy * 2 + kk

    to_x = (x_other, space)
    to_y = (x, place(z, y_other, core))
    to_p = (x, place(z, y, 1 - core))
    to_grad = [(line, flip) for flip in range(2) for line in range(lines)]

    barrier = pltpu.get_barrier_semaphore()
    pl.semaphore_signal(barrier, inc=1, device_id=to_x, device_id_type=MESH)
    pl.semaphore_signal(barrier, inc=1, device_id=to_p, device_id_type=MESH)
    pl.semaphore_signal(barrier, inc=1, device_id=to_y, device_id_type=MESH)
    for line in order[1:]:
        for yy in (y, y_other):
            pl.semaphore_signal(
                barrier, inc=1, device_id=(x, place(line, yy, core)), device_id_type=MESH
            )
    low = images // 2

    def region(group, line, yy, kk):
        return maps.at[pl.ds(group * images, images), pl.ds(1 + place(line, yy, kk) * rows, rows)]

    def copy(src, dst, send, recv, to):
        return pltpu.make_async_remote_copy(
            src_ref=src, dst_ref=dst, send_sem=send, recv_sem=recv,
            device_id=to, device_id_type=MESH,
        )

    maps[pl.ds(x * images, images), pl.ds(1 + space * rows, rows)] = act[...]
    zeros = jnp.zeros((maps.shape[0], 1, columns, channels), maps.dtype)
    maps[:, 0:1] = zeros
    maps[:, height + 1 : height + 2] = zeros
    acc[...] = jnp.zeros_like(acc)
    gbuf[0] = grad[...].reshape(gbuf.shape[1:])
    pl.semaphore_wait(barrier, 9)

    own = region(x, z, y, core)
    x_copy = [copy(region(x, line, y, core), region(x, line, y, core), sx.at[n], rx.at[n], to_x)
              for n, line in enumerate(order)]
    y_copy = [copy(region(x, line, y, core), region(x, line, y, core), sy.at[n], ry.at[n], to_y)
              for n, line in enumerate(order)]
    dy_copy, dx_copy, p_copy = [], [], []
    for n, line in enumerate(order):
        from_x = maps.at[pl.ds(x_other * images, low), pl.ds(1 + place(line, y, core) * rows, rows)]
        from_y = maps.at[pl.ds(x * images + low, images - low),
                         pl.ds(1 + place(line, y_other, core) * rows, rows)]
        dy_copy.append(copy(from_x, from_x, sdy.at[n], rdy.at[n], to_y))
        dx_copy.append(copy(from_y, from_y, sdx.at[n], rdx.at[n], to_x))
        pair = []
        for m, yy in enumerate((y, y_other)):
            whole = maps.at[:, pl.ds(1 + place(line, yy, core) * rows, rows)]
            pair.append(copy(whole, whole, sp.at[n, m], rp.at[n, m], to_p))
        p_copy.append(pair)
    z_copy = [copy(own, own, sz.at[line], rz.at[z], (x, place(line, y, core))) for line in order[1:]]
    z_wait = [copy(region(x, line, y, core), region(x, line, y, core), sz.at[line], rz.at[line],
                   (x, place(line, y, core))) for line in order[1:]]

    x_copy[0].start()
    y_copy[0].start()
    for one in z_copy:
        one.start()
    gx = copy(gbuf.at[0], gbuf.at[1], sg.at[0], rg.at[0], to_x)
    gp0 = copy(gbuf.at[0], gbuf.at[2], sg.at[1], rg.at[1], to_p)
    gp1 = copy(gbuf.at[1], gbuf.at[3], sg.at[2], rg.at[2], to_p)
    gp0.start()
    gx.start()

    def forward_first(n):
        x_copy[n].wait_recv()
        dy_copy[n].start()
        y_copy[n].wait_recv()
        dx_copy[n].start()
        p_copy[n][0].start()

    def forward_second(n):
        dy_copy[n].wait_recv()
        dx_copy[n].wait_recv()
        p_copy[n][1].start()

    def forward_line(n):
        z_wait[n - 1].wait_recv()
        x_copy[n].start()
        y_copy[n].start()

    def wait_partner(n):
        p_copy[n][0].wait_recv()
        p_copy[n][1].wait_recv()

    forward_first(0)
    forward_line(1)
    gx.wait_recv()
    gp1.start()
    forward_line(2)
    forward_first(1)
    forward_second(0)
    forward_line(3)

    gp0.wait_recv()
    gp1.wait_recv()
    flat = gbuf[...].reshape(-1, channels)
    product = lax.dot_general(
        flat, flat, (((0,), (0,)), ((), ())), preferred_element_type=jnp.float32
    )
    gpart[...] = product.reshape(gpart.shape)
    grad_copies = []
    for n, line in enumerate(order):
        for m, yy in enumerate((y, y_other)):
            if n == 0 and m == 0:
                continue
            index = 2 * n + m
            one = copy(gpart.at[place(line, yy, core)], grecv.at[2 * z + y],
                       ss.at[index], rs.at[2 * z + y], (x, place(line, yy, core)))
            one.start()
            got = copy(gpart.at[place(line, yy, core)], grecv.at[2 * line + yy],
                       ss.at[index], rs.at[2 * line + yy], (x, place(line, yy, core)))
            grad_copies.append((one, got))

    me = x * spaces + space
    first = me * share
    tap_first = first // channels
    r = lax.broadcasted_iota(jnp.int32, (share, channels), 0) + first % channels
    c = lax.broadcasted_iota(jnp.int32, (share, channels), 1)
    select = [
        jnp.where(r == c, 1.0, 0.0).astype(maps.dtype),
        jnp.where(r == c + channels, 1.0, 0.0).astype(maps.dtype),
    ]
    taps = [tap_first, jnp.minimum(tap_first + 1, TAPS * TAPS - 1)]
    depth = 4 * rows
    width = depth * columns
    j = lax.broadcasted_iota(jnp.int32, (share, width), 1) % columns
    blocks = maps.shape[0]

    def right_of(image, row):
        return maps[image, pl.ds(row, depth)].reshape(width, channels)

    def chunk(image, line):
        start = 1 + line * depth
        left = None
        for u in range(2):
            dy, dx = taps[u] // TAPS - 1, taps[u] % TAPS - 1
            z_u = lax.dot_general(
                select[u], right_of(image, start + dy), (((1,), (1,)), ((), ())),
                preferred_element_type=jnp.float32,
            )
            z_u = pltpu.roll(z_u, (width - dx) % width, 1)
            z_u = jnp.where((j + dx >= 0) & (j + dx < columns), z_u, 0.0)
            left = z_u if left is None else left + z_u
        low_shift = jnp.where(j < columns - 1, pltpu.roll(left, width - 1, 1), 0.0)
        high_shift = jnp.where(j > 0, pltpu.roll(left, 1, 1), 0.0)
        stacked = jnp.concatenate([low_shift, left, high_shift], axis=0).astype(maps.dtype)
        for ky in range(TAPS):
            acc[ky] += jnp.dot(
                stacked, right_of(image, start + ky - 1), preferred_element_type=jnp.float32
            )

    def chunks(line_a, line_b):
        def body(step, carry):
            line = jnp.where(step < blocks, line_a, line_b)
            chunk(step % blocks, line)
            return carry

        lax.fori_loop(0, 2 * blocks, body, 0)

    forward_first(2)
    forward_second(1)
    wait_partner(0)
    wait_partner(1)
    forward_first(3)
    forward_second(2)
    wait_partner(2)
    forward_second(3)
    chunks(3 * half, 1 + half)
    wait_partner(3)
    chunks(3 - 3 * half, 2 - half)

    for ky in range(TAPS):
        for kx in range(TAPS):
            at = (TAPS * ky + kx) * channels
            sums[:, at : at + channels] = acc[ky, kx * share : (kx + 1) * share, :]
    total = gpart[space]
    for one, got in grad_copies:
        got.wait_recv()
    for n, line in enumerate(order):
        for m, yy in enumerate((y, y_other)):
            if n == 0 and m == 0:
                continue
            total = total + grecv[2 * line + yy]
    grad_sum[...] = total

    for one, got in grad_copies:
        one.wait_send()
    for one in x_copy + y_copy + dx_copy + dy_copy + z_copy + [gx, gp0, gp1]:
        one.wait_send()
    for pair in p_copy:
        pair[0].wait_send()
        pair[1].wait_send()


def kernel_form(activations, out_grads, old_input_factor, old_grad_factor):
    images, rows, columns, channels = activations.shape
    groups = lax.axis_size("dp")
    spaces = lax.axis_size("space")
    lines = spaces // 4
    height = rows * spaces
    positions = images * groups * height * columns
    share, width_all = old_input_factor.shape
    grad_share = old_grad_factor.shape[0]
    dma = pltpu.SemaphoreType.DMA
    vmem = pl.BlockSpec(memory_space=pltpu.VMEM)
    here = images * rows * columns
    input_sum, grad_sum = pl.pallas_call(
        gather_kernel,
        out_shape=(
            jax.ShapeDtypeStruct((share, width_all), jnp.float32),
            jax.ShapeDtypeStruct((grad_share, channels), jnp.float32),
        ),
        in_specs=[vmem, vmem],
        out_specs=(vmem, vmem),
        scratch_shapes=[
            pltpu.VMEM((images * groups, height + 2, columns, channels), activations.dtype),
            pltpu.VMEM((TAPS, TAPS * share, channels), jnp.float32),
            pltpu.VMEM((4, here, channels), out_grads.dtype),
            pltpu.VMEM((spaces, grad_share, channels), jnp.float32),
            pltpu.VMEM((2 * lines, grad_share, channels), jnp.float32),
        ]
        + [dma((lines,))] * 10
        + [dma((lines, 2))] * 2
        + [dma((3,))] * 2
        + [dma((2 * lines,))] * 2,
        compiler_params=pltpu.CompilerParams(
            collective_id=0, has_side_effects=True, vmem_limit_bytes=24 * 2**20
        ),
        cost_estimate=pl.CostEstimate(
            flops=2 * positions * share * width_all, bytes_accessed=4 * share * width_all,
            transcendentals=0,
        ),
    )(activations, out_grads)
    input_factor = 0.5 * old_input_factor.astype(jnp.float32) + 0.5 / positions * input_sum
    grad_factor = 0.5 * old_grad_factor + 0.5 / positions * grad_sum
    return input_factor, grad_factor


def per_device(activations, out_grads, old_input_factor, old_grad_factor):
    groups, spaces = lax.axis_size("dp"), lax.axis_size("space")
    images, channels = activations.shape[0], activations.shape[3]
    whole_map = activations.size * groups * spaces
    small = whole_map <= old_input_factor.shape[1] ** 2
    fits = groups == 2 and spaces == 16 and images % 2 == 0 and old_input_factor.shape[0] <= channels
    form = kernel_form if small and fits else reduced_form
    return form(activations, out_grads, old_input_factor, old_grad_factor)


def solution(mesh):
    return jax.shard_map(
        per_device,
        mesh=mesh,
        in_specs=(
            P("dp", "space", None, None),
            P("dp", "space", None, None),
            P(("dp", "space"), None),
            P("space", None),
        ),
        out_specs=(P(("dp", "space"), None), P("space", None)),
        check_vma=False,
    )
```

profile of v0, /device:TPU:0, one launch (start us, length us, event | category | flops | bytes accessed | tf_op | source)
XLA Modules:
  0.0 34.7 jit_solution(5125522930936506076)
XLA Ops:
  0.6 0.0 copy-start
  0.6 0.8 %copy-done = bf16[2,1,64,256]{3,2,1,0:T(8,128)(2,1)S(1)} copy-done((bf16[2,1,64,256]{3,2,1,0:T(8,128)(2,1)S(1)}, bf16[2,1,64,256]{3,2,1,0:T(8,128)(2,1)}, u32[]{:S(2)}) %copy-start) | copy-done | bytes 65560
  1.5 0.0 copy-start.1
  1.5 0.8 %copy-done.1 = bf16[2,1,64,256]{3,2,1,0:T(8,128)(2,1)S(1)} copy-done((bf16[2,1,64,256]{3,2,1,0:T(8,128)(2,1)S(1)}, bf16[2,1,64,256]{3,2,1,0:T(8,128)(2,1)}, u32[]{:S(2)}) %copy-start.1) | copy-done | bytes 65560
  2.3 0.0 copy-start.2
  2.3 30.8 %shard_map.59 = (f32[72,2304]{1,0:T(8,128)S(1)}, f32[16,256]{1,0:T(8,128)S(1)}) custom-call(bf16[2,1,64,256]{3,2,1,0:T(8,128)(2,1)S(1)} %copy-done, bf16[2,1,64,256]{3,2,1,0:T(8,128)(2,1)S(1)} %copy-done.1), custom_call_target="tpu_custom_call" | custom-call | flops 1358954496 | bytes 663552 | tf_op jit(solution)/shard_map/pallas_call | solution.py:316
  33.2 0.0 copy-done.2
  33.2 0.0 copy-start.3
  33.2 0.9 %multiply_add_fusion = f32[72,2304]{1,0:T(8,128)} fusion(f32[72,2304]{1,0:T(8,128)S(1)} %get-tuple-element.4, bf16[72,2304]{1,0:T(8,128)(2,1)S(1)} %copy-done.2), kind=kLoop, calls=%fused_computation | loop fusion | flops 663552 | bytes 1658880 | tf_op jit(solution)/shard_map/add | solution.py:343
  34.1 0.0 copy-done.3
  34.1 0.6 %multiply_add_fusion.1 = f32[16,256]{1,0:T(8,128)} fusion(f32[16,256]{1,0:T(8,128)S(1)} %get-tuple-element.5, f32[16,256]{1,0:T(8,128)S(1)} %copy-done.3), kind=kLoop, calls=%fused_computation.1 | loop fusion | flops 12288 | bytes 49152 | tf_op jit(solution)/shard_map/add | solution.py:344
Async XLA Ops:
  0.6 0.8 %copy-start = (bf16[2,1,64,256]{3,2,1,0:T(8,128)(2,1)S(1)}, bf16[2,1,64,256]{3,2,1,0:T(8,128)(2,1)}, u32[]{:S(2)}) copy-start(bf16[2,1,64,256]{3,2,1,0:T(8,128)(2,1)} %act.1) | copy-start | bytes 196612
  1.5 0.8 %copy-start.1 = (bf16[2,1,64,256]{3,2,1,0:T(8,128)(2,1)S(1)}, bf16[2,1,64,256]{3,2,1,0:T(8,128)(2,1)}, u32[]{:S(2)}) copy-start(bf16[2,1,64,256]{3,2,1,0:T(8,128)(2,1)} %grad.1) | copy-start | bytes 196612
  2.3 30.8 %copy-start.2 = (bf16[72,2304]{1,0:T(8,128)(2,1)S(1)}, bf16[72,2304]{1,0:T(8,128)(2,1)}, u32[]{:S(2)}) copy-start(bf16[72,2304]{1,0:T(8,128)(2,1)} %param.6) | copy-start | bytes 995332
  33.2 1.0 %copy-start.3 = (f32[16,256]{1,0:T(8,128)S(1)}, f32[16,256]{1,0:T(8,128)}, u32[]{:S(2)}) copy-start(f32[16,256]{1,0:T(8,128)} %param.7) | copy-start | bytes 49156
where the time goes:
time: 35 us; the launch traced here: 34.7 us
  Pallas kernels  30.8 us (88%)
  local copies, waits for them, and re-layouts  1.68 us (5%)
  other arithmetic  1.55 us (4%)
  between operations  0.66 us (2%)
    pallas_call x1, Pallas kernels, kernel_form(): pl.pallas_call(gather_kernel, out_shape=(jax.ShapeDtypeStruct((share, wid...  30.8 us
    unnamed x8, local copies, waits for them, and re-layouts  1.68 us
    add x1, other arithmetic, kernel_form(): 0.5 * old_input_factor.astype(jnp.float32) + 0.5 / positions * input_sum  0.94 us

commit v1 on v0

--- a/solution.py
+++ b/solution.py
@@ -87,7 +87,7 @@
 TAPS = 3
 
 
-def gather_kernel(act, grad, sums, grad_sum, maps, acc, gbuf, gpart, grecv,
+def gather_kernel(act, grad, sums, grad_sum, maps, gbuf, gpart, grecv, here_sem,
                   sz, rz, sx, rx, sy, ry, sdx, rdx, sdy, rdy, sp, rp, sg, rg, ss, rs):
     images, rows, columns, channels = act.shape
     share = sums.shape[0]
@@ -131,18 +131,19 @@
             device_id=to, device_id_type=MESH,
         )
 
-    maps[pl.ds(x * images, images), pl.ds(1 + space * rows, rows)] = act[...]
+    own = region(x, z, y, core)
+    keep = pltpu.make_async_copy(act, own, here_sem.at[0])
+    keep_grad = pltpu.make_async_copy(grad, gbuf.at[0], here_sem.at[1])
+    keep.start()
+    keep_grad.start()
     zeros = jnp.zeros((maps.shape[0], 1, columns, channels), maps.dtype)
     maps[:, 0:1] = zeros
     maps[:, height + 1 : height + 2] = zeros
-    acc[...] = jnp.zeros_like(acc)
-    gbuf[0] = grad[...].reshape(gbuf.shape[1:])
     pl.semaphore_wait(barrier, 9)
 
-    own = region(x, z, y, core)
-    x_copy = [copy(region(x, line, y, core), region(x, line, y, core), sx.at[n], rx.at[n], to_x)
+    x_copy = [copy(region(x, line, y, core) if n else act, region(x, line, y, core), sx.at[n], rx.at[n], to_x)
               for n, line in enumerate(order)]
-    y_copy = [copy(region(x, line, y, core), region(x, line, y, core), sy.at[n], ry.at[n], to_y)
+    y_copy = [copy(region(x, line, y, core) if n else act, region(x, line, y, core), sy.at[n], ry.at[n], to_y)
               for n, line in enumerate(order)]
     dy_copy, dx_copy, p_copy = [], [], []
     for n, line in enumerate(order):
@@ -156,7 +157,7 @@
             whole = maps.at[:, pl.ds(1 + place(line, yy, core) * rows, rows)]
             pair.append(copy(whole, whole, sp.at[n, m], rp.at[n, m], to_p))
         p_copy.append(pair)
-    z_copy = [copy(own, own, sz.at[line], rz.at[z], (x, place(line, y, core))) for line in order[1:]]
+    z_copy = [copy(act, own, sz.at[line], rz.at[z], (x, place(line, y, core))) for line in order[1:]]
     z_wait = [copy(region(x, line, y, core), region(x, line, y, core), sz.at[line], rz.at[line],
                    (x, place(line, y, core))) for line in order[1:]]
 
@@ -164,8 +165,8 @@
     y_copy[0].start()
     for one in z_copy:
         one.start()
-    gx = copy(gbuf.at[0], gbuf.at[1], sg.at[0], rg.at[0], to_x)
-    gp0 = copy(gbuf.at[0], gbuf.at[2], sg.at[1], rg.at[1], to_p)
+    gx = copy(grad, gbuf.at[1], sg.at[0], rg.at[0], to_x)
+    gp0 = copy(grad, gbuf.at[2], sg.at[1], rg.at[1], to_p)
     gp1 = copy(gbuf.at[1], gbuf.at[3], sg.at[2], rg.at[2], to_p)
     gp0.start()
     gx.start()
@@ -191,15 +192,17 @@
         p_copy[n][0].wait_recv()
         p_copy[n][1].wait_recv()
 
+    keep.wait()
     forward_first(0)
     forward_line(1)
     gx.wait_recv()
     gp1.start()
     forward_line(2)
+    forward_second(0)
     forward_first(1)
-    forward_second(0)
     forward_line(3)
 
+    keep_grad.wait()
     gp0.wait_recv()
     gp1.wait_recv()
     flat = gbuf[...].reshape(-1, channels)
@@ -225,63 +228,66 @@
     tap_first = first // channels
     r = lax.broadcasted_iota(jnp.int32, (share, channels), 0) + first % channels
     c = lax.broadcasted_iota(jnp.int32, (share, channels), 1)
-    select = [
-        jnp.where(r == c, 1.0, 0.0).astype(maps.dtype),
-        jnp.where(r == c + channels, 1.0, 0.0).astype(maps.dtype),
-    ]
-    taps = [tap_first, jnp.minimum(tap_first + 1, TAPS * TAPS - 1)]
-    depth = 4 * rows
-    width = depth * columns
-    j = lax.broadcasted_iota(jnp.int32, (share, width), 1) % columns
+    select = jnp.concatenate(
+        [jnp.where(r == c, 1.0, 0.0), jnp.where(r == c + channels, 1.0, 0.0)], axis=1
+    ).astype(maps.dtype)
+    tap_next = jnp.minimum(tap_first + 1, TAPS * TAPS - 1)
+    edge = channels - first % channels
     blocks = maps.shape[0]
 
-    def right_of(image, row):
-        return maps[image, pl.ds(row, depth)].reshape(width, channels)
-
-    def chunk(image, line):
-        start = 1 + line * depth
-        left = None
-        for u in range(2):
-            dy, dx = taps[u] // TAPS - 1, taps[u] % TAPS - 1
-            z_u = lax.dot_general(
-                select[u], right_of(image, start + dy), (((1,), (1,)), ((), ())),
-                preferred_element_type=jnp.float32,
-            )
-            z_u = pltpu.roll(z_u, (width - dx) % width, 1)
-            z_u = jnp.where((j + dx >= 0) & (j + dx < columns), z_u, 0.0)
-            left = z_u if left is None else left + z_u
-        low_shift = jnp.where(j < columns - 1, pltpu.roll(left, width - 1, 1), 0.0)
-        high_shift = jnp.where(j > 0, pltpu.roll(left, 1, 1), 0.0)
-        stacked = jnp.concatenate([low_shift, left, high_shift], axis=0).astype(maps.dtype)
+    def stage(start, depth):
+        width = blocks * depth * columns
+        row = lax.broadcasted_iota(jnp.int32, (share, width), 0)
+        j = lax.broadcasted_iota(jnp.int32, (share, width), 1) % columns
+        shift = jnp.where(row < edge, tap_first % TAPS, tap_next % TAPS) - 1
+
+        def right_of(move):
+            return maps[:, pl.ds(1 + start + move, depth)].reshape(width, channels)
+
+        both = jnp.concatenate(
+            [right_of(tap_first // TAPS - 1), right_of(tap_next // TAPS - 1)], axis=1
+        )
+        picked = lax.dot_general(
+            select, both, (((1,), (1,)), ((), ())), preferred_element_type=jnp.float32
+        )
+
+        def lower(value):
+            return jnp.where(j < columns - 1, pltpu.roll(value, width - 1, 1), 0.0)
+
+        def higher(value):
+            return jnp.where(j > 0, pltpu.roll(value, 1, 1), 0.0)
+
+        left = jnp.where(
+            shift == 0, picked, jnp.where(shift > 0, lower(picked), higher(picked))
+        )
+        stacked = jnp.concatenate([lower(left), left, higher(left)], axis=0).astype(maps.dtype)
         for ky in range(TAPS):
-            acc[ky] += jnp.dot(
-                stacked, right_of(image, start + ky - 1), preferred_element_type=jnp.float32
-            )
-
-    def chunks(line_a, line_b):
-        def body(step, carry):
-            line = jnp.where(step < blocks, line_a, line_b)
-            chunk(step % blocks, line)
-            return carry
-
-        lax.fori_loop(0, 2 * blocks, body, 0)
-
+            part = jnp.dot(stacked, right_of(ky - 1), preferred_element_type=jnp.float32)
+            for kx in range(TAPS):
+                at = (TAPS * ky + kx) * channels
+                piece = part[kx * share : (kx + 1) * share]
+                if fresh[0]:
+                    sums[:, at : at + channels] = piece
+                else:
+                    sums[:, at : at + channels] += piece
+        fresh[0] = False
+
+    fresh = [True]
+    line_rows = 4 * rows
+    side = line_rows + line_rows // 2
     forward_first(2)
     forward_second(1)
     wait_partner(0)
     wait_partner(1)
+    stage(half * (height - side), side)
     forward_first(3)
     forward_second(2)
     wait_partner(2)
+    stage(side, height - 2 * side)
     forward_second(3)
-    chunks(3 * half, 1 + half)
     wait_partner(3)
-    chunks(3 - 3 * half, 2 - half)
-
-    for ky in range(TAPS):
-        for kx in range(TAPS):
-            at = (TAPS * ky + kx) * channels
-            sums[:, at : at + channels] = acc[ky, kx * share : (kx + 1) * share, :]
+    stage((1 - half) * (height - side), side)
+
     total = gpart[space]
     for one, got in grad_copies:
         got.wait_recv()
@@ -312,22 +318,22 @@
     grad_share = old_grad_factor.shape[0]
     dma = pltpu.SemaphoreType.DMA
     vmem = pl.BlockSpec(memory_space=pltpu.VMEM)
-    here = images * rows * columns
+    hbm = pl.BlockSpec(memory_space=pltpu.HBM)
     input_sum, grad_sum = pl.pallas_call(
         gather_kernel,
         out_shape=(
             jax.ShapeDtypeStruct((share, width_all), jnp.float32),
             jax.ShapeDtypeStruct((grad_share, channels), jnp.float32),
         ),
-        in_specs=[vmem, vmem],
+        in_specs=[hbm, hbm],
         out_specs=(vmem, vmem),
         scratch_shapes=[
             pltpu.VMEM((images * groups, height + 2, columns, channels), activations.dtype),
-            pltpu.VMEM((TAPS, TAPS * share, channels), jnp.float32),
-            pltpu.VMEM((4, here, channels), out_grads.dtype),
+            pltpu.VMEM((4,) + out_grads.shape, out_grads.dtype),
             pltpu.VMEM((spaces, grad_share, channels), jnp.float32),
             pltpu.VMEM((2 * lines, grad_share, channels), jnp.float32),
         ]
+        + [dma((2,))]
         + [dma((lines,))] * 10
         + [dma((lines, 2))] * 2
         + [dma((3,))] * 2

time: 35 us -> 30.7 us (0.88)
  Pallas kernels: 30.8 us -> 26.6 us
    pallas_call x1, Pallas kernels: 30.8 us -> 26.6 us  [kernel_form(): pl.pallas_call(gather_kernel, out_shape=(jax.ShapeDtypeStruct((share, wid...]
where the time goes in v1:
time: 30.7 us; the launch traced here: 30.5 us
  Pallas kernels  26.6 us (87%)
  local copies, waits for them, and re-layouts  1.68 us (5%)
  other arithmetic  1.55 us (5%)
  between operations  0.66 us (2%)
    pallas_call x1, Pallas kernels, kernel_form(): pl.pallas_call(gather_kernel, out_shape=(jax.ShapeDtypeStruct((share, wid...  26.6 us
    unnamed x8, local copies, waits for them, and re-layouts  1.68 us
    add x1, other arithmetic, kernel_form(): 0.5 * old_input_factor.astype(jnp.float32) + 0.5 / positions * input_sum  0.94 us

profile of v1, /device:TPU:0, one launch (start us, length us, event | category | flops | bytes accessed | tf_op | source)
XLA Modules:
  0.0 30.5 jit_solution(6934356340007446102)
XLA Ops:
  0.6 0.0 copy-start
  0.6 0.8 %copy-done = bf16[2,1,64,256]{3,2,1,0:T(8,128)(2,1)S(1)} copy-done((bf16[2,1,64,256]{3,2,1,0:T(8,128)(2,1)S(1)}, bf16[2,1,64,256]{3,2,1,0:T(8,128)(2,1)}, u32[]{:S(2)}) %copy-start) | copy-done | bytes 65560
  1.5 0.0 copy-start.1
  1.5 0.8 %copy-done.1 = bf16[2,1,64,256]{3,2,1,0:T(8,128)(2,1)S(1)} copy-done((bf16[2,1,64,256]{3,2,1,0:T(8,128)(2,1)S(1)}, bf16[2,1,64,256]{3,2,1,0:T(8,128)(2,1)}, u32[]{:S(2)}) %copy-start.1) | copy-done | bytes 65560
  2.3 0.0 copy-start.2
  2.3 26.6 %shard_map.59 = (f32[72,2304]{1,0:T(8,128)S(1)}, f32[16,256]{1,0:T(8,128)S(1)}) custom-call(bf16[2,1,64,256]{3,2,1,0:T(8,128)(2,1)S(1)} %copy-done, bf16[2,1,64,256]{3,2,1,0:T(8,128)(2,1)S(1)} %copy-done.1), custom_call_target="tpu_custom_call" | custom-call | flops 1358954496 | bytes 663552 | tf_op jit(solution)/shard_map/pallas_call | solution.py:322
  28.9 0.0 copy-done.2
  28.9 0.0 copy-start.3
  29.0 0.9 %multiply_add_fusion = f32[72,2304]{1,0:T(8,128)} fusion(f32[72,2304]{1,0:T(8,128)S(1)} %get-tuple-element.4, bf16[72,2304]{1,0:T(8,128)(2,1)S(1)} %copy-done.2), kind=kLoop, calls=%fused_computation | loop fusion | flops 663552 | bytes 1658880 | tf_op jit(solution)/shard_map/add | solution.py:349
  29.9 0.0 copy-done.3
  29.9 0.6 %multiply_add_fusion.1 = f32[16,256]{1,0:T(8,128)} fusion(f32[16,256]{1,0:T(8,128)S(1)} %get-tuple-element.5, f32[16,256]{1,0:T(8,128)S(1)} %copy-done.3), kind=kLoop, calls=%fused_computation.1 | loop fusion | flops 12288 | bytes 49152 | tf_op jit(solution)/shard_map/add | solution.py:350
Async XLA Ops:
  0.6 0.8 %copy-start = (bf16[2,1,64,256]{3,2,1,0:T(8,128)(2,1)S(1)}, bf16[2,1,64,256]{3,2,1,0:T(8,128)(2,1)}, u32[]{:S(2)}) copy-start(bf16[2,1,64,256]{3,2,1,0:T(8,128)(2,1)} %act.1) | copy-start | bytes 196612
  1.5 0.8 %copy-start.1 = (bf16[2,1,64,256]{3,2,1,0:T(8,128)(2,1)S(1)}, bf16[2,1,64,256]{3,2,1,0:T(8,128)(2,1)}, u32[]{:S(2)}) copy-start(bf16[2,1,64,256]{3,2,1,0:T(8,128)(2,1)} %grad.1) | copy-start | bytes 196612
  2.3 26.6 %copy-start.2 = (bf16[72,2304]{1,0:T(8,128)(2,1)S(1)}, bf16[72,2304]{1,0:T(8,128)(2,1)}, u32[]{:S(2)}) copy-start(bf16[72,2304]{1,0:T(8,128)(2,1)} %param.6) | copy-start | bytes 995332
  28.9 1.0 %copy-start.3 = (f32[16,256]{1,0:T(8,128)S(1)}, f32[16,256]{1,0:T(8,128)}, u32[]{:S(2)}) copy-start(f32[16,256]{1,0:T(8,128)} %param.7) | copy-start | bytes 49156

commit v2 on v1

--- a/solution.py
+++ b/solution.py
@@ -109,17 +109,21 @@
     to_x = (x_other, space)
     to_y = (x, place(z, y_other, core))
     to_p = (x, place(z, y, 1 - core))
-    to_grad = [(line, flip) for flip in range(2) for line in range(lines)]
 
     barrier = pltpu.get_barrier_semaphore()
     pl.semaphore_signal(barrier, inc=1, device_id=to_x, device_id_type=MESH)
     pl.semaphore_signal(barrier, inc=1, device_id=to_p, device_id_type=MESH)
     pl.semaphore_signal(barrier, inc=1, device_id=to_y, device_id_type=MESH)
-    for line in order[1:]:
-        for yy in (y, y_other):
-            pl.semaphore_signal(
-                barrier, inc=1, device_id=(x, place(line, yy, core)), device_id_type=MESH
-            )
+    middle = (z % 3 + 1) // 2
+    is_middle = middle == 1
+    near = (x, place(jnp.where(is_middle, 3 * half, 1 + half), y, core))
+    across = (x, place(3 - z, y, core))
+    pl.semaphore_signal(barrier, inc=1, device_id=near, device_id_type=MESH)
+
+    @pl.when(is_middle)
+    def _():
+        pl.semaphore_signal(barrier, inc=1, device_id=across, device_id_type=MESH)
+
     low = images // 2
 
     def region(group, line, yy, kk):
@@ -139,7 +143,7 @@
     zeros = jnp.zeros((maps.shape[0], 1, columns, channels), maps.dtype)
     maps[:, 0:1] = zeros
     maps[:, height + 1 : height + 2] = zeros
-    pl.semaphore_wait(barrier, 9)
+    pl.semaphore_wait(barrier, 4 + middle)
 
     x_copy = [copy(region(x, line, y, core) if n else act, region(x, line, y, core), sx.at[n], rx.at[n], to_x)
               for n, line in enumerate(order)]
@@ -157,14 +161,26 @@
             whole = maps.at[:, pl.ds(1 + place(line, yy, core) * rows, rows)]
             pair.append(copy(whole, whole, sp.at[n, m], rp.at[n, m], to_p))
         p_copy.append(pair)
-    z_copy = [copy(act, own, sz.at[line], rz.at[z], (x, place(line, y, core))) for line in order[1:]]
-    z_wait = [copy(region(x, line, y, core), region(x, line, y, core), sz.at[line], rz.at[line],
-                   (x, place(line, y, core))) for line in order[1:]]
+    def z_block(n):
+        return act if n == 0 else region(x, order[n], y, core)
+
+    def z_send(n, to, slot):
+        return copy(z_block(n), region(x, order[n], y, core), sz.at[slot], rz.at[order[n]], to)
+
+    z_near = z_send(0, near, 0)
+    z_across = z_send(0, across, 1)
+    z_pass = {1: z_send(1, across, 2), 2: z_send(2, near, 3), 3: z_send(3, near, 4)}
+    z_wait = [copy(region(x, line, y, core), region(x, line, y, core), sz.at[0], rz.at[line], near)
+              for line in order[1:]]
 
     x_copy[0].start()
     y_copy[0].start()
-    for one in z_copy:
-        one.start()
+    z_near.start()
+
+    @pl.when(is_middle)
+    def _():
+        z_across.start()
+
     gx = copy(grad, gbuf.at[1], sg.at[0], rg.at[0], to_x)
     gp0 = copy(grad, gbuf.at[2], sg.at[1], rg.at[1], to_p)
     gp1 = copy(gbuf.at[1], gbuf.at[3], sg.at[2], rg.at[2], to_p)
@@ -185,6 +201,11 @@
 
     def forward_line(n):
         z_wait[n - 1].wait_recv()
+
+        @pl.when(is_middle)
+        def _():
+            z_pass[n].start()
+
         x_copy[n].start()
         y_copy[n].start()
 
@@ -210,6 +231,64 @@
         flat, flat, (((0,), (0,)), ((), ())), preferred_element_type=jnp.float32
     )
     gpart[...] = product.reshape(gpart.shape)
+    me = x * spaces + space
+    first = me * share
+    tap_first = first // channels
+    r = lax.broadcasted_iota(jnp.int32, (share, channels), 0) + first % channels
+    c = lax.broadcasted_iota(jnp.int32, (share, channels), 1)
+    select = jnp.concatenate(
+        [jnp.where(r == c, 1.0, 0.0), jnp.where(r == c + channels, 1.0, 0.0)], axis=1
+    ).astype(maps.dtype)
+    tap_next = jnp.minimum(tap_first + 1, TAPS * TAPS - 1)
+    edge = channels - first % channels
+    blocks = maps.shape[0]
+
+    def stage(start, depth):
+        width = blocks * depth * columns
+        row = lax.broadcasted_iota(jnp.int32, (share, width), 0)
+        j = lax.broadcasted_iota(jnp.int32, (share, width), 1) % columns
+        shift = jnp.where(row < edge, tap_first % TAPS, tap_next % TAPS) - 1
+
+        def right_of(move):
+            return maps[:, pl.ds(1 + start + move, depth)].reshape(width, channels)
+
+        both = jnp.concatenate(
+            [right_of(tap_first // TAPS - 1), right_of(tap_next // TAPS - 1)], axis=1
+        )
+        picked = lax.dot_general(
+            select, both, (((1,), (1,)), ((), ())), preferred_element_type=jnp.float32
+        )
+
+        def lower(value):
+            return jnp.where(j < columns - 1, pltpu.roll(value, width - 1, 1), 0.0)
+
+        def higher(value):
+            return jnp.where(j > 0, pltpu.roll(value, 1, 1), 0.0)
+
+        left = jnp.where(
+            shift == 0, picked, jnp.where(shift > 0, lower(picked), higher(picked))
+        )
+        stacked = jnp.concatenate([lower(left), left, higher(left)], axis=0).astype(maps.dtype)
+        for ky in range(TAPS):
+            part = jnp.dot(stacked, right_of(ky - 1), preferred_element_type=jnp.float32)
+            for kx in range(TAPS):
+                at = (TAPS * ky + kx) * channels
+                piece = part[kx * share : (kx + 1) * share]
+                if fresh[0]:
+                    sums[:, at : at + channels] = piece
+                else:
+                    sums[:, at : at + channels] += piece
+        fresh[0] = False
+
+    fresh = [True]
+    line_rows = 4 * rows
+    side = line_rows + line_rows // 2
+    forward_first(2)
+    forward_second(1)
+    wait_partner(0)
+    wait_partner(1)
+    stage(half * (height - side), side)
+    forward_first(3)
     grad_copies = []
     for n, line in enumerate(order):
         for m, yy in enumerate((y, y_other)):
@@ -223,64 +302,6 @@
                        ss.at[index], rs.at[2 * line + yy], (x, place(line, yy, core)))
             grad_copies.append((one, got))
 
-    me = x * spaces + space
-    first = me * share
-    tap_first = first // channels
-    r = lax.broadcasted_iota(jnp.int32, (share, channels), 0) + first % channels
-    c = lax.broadcasted_iota(jnp.int32, (share, channels), 1)
-    select = jnp.concatenate(
-        [jnp.where(r == c, 1.0, 0.0), jnp.where(r == c + channels, 1.0, 0.0)], axis=1
-    ).astype(maps.dtype)
-    tap_next = jnp.minimum(tap_first + 1, TAPS * TAPS - 1)
-    edge = channels - first % channels
-    blocks = maps.shape[0]
-
-    def stage(start, depth):
-        width = blocks * depth * columns
-        row = lax.broadcasted_iota(jnp.int32, (share, width), 0)
-        j = lax.broadcasted_iota(jnp.int32, (share, width), 1) % columns
-        shift = jnp.where(row < edge, tap_first % TAPS, tap_next % TAPS) - 1
-
-        def right_of(move):
-            return maps[:, pl.ds(1 + start + move, depth)].reshape(width, channels)
-
-        both = jnp.concatenate(
-            [right_of(tap_first // TAPS - 1), right_of(tap_next // TAPS - 1)], axis=1
-        )
-        picked = lax.dot_general(
-            select, both, (((1,), (1,)), ((), ())), preferred_element_type=jnp.float32
-        )
-
-        def lower(value):
-            return jnp.where(j < columns - 1, pltpu.roll(value, width - 1, 1), 0.0)
-
-        def higher(value):
-            return jnp.where(j > 0, pltpu.roll(value, 1, 1), 0.0)
-
-        left = jnp.where(
-            shift == 0, picked, jnp.where(shift > 0, lower(picked), higher(picked))
-        )
-        stacked = jnp.concatenate([lower(left), left, higher(left)], axis=0).astype(maps.dtype)
-        for ky in range(TAPS):
-            part = jnp.dot(stacked, right_of(ky - 1), preferred_element_type=jnp.float32)
-            for kx in range(TAPS):
-                at = (TAPS * ky + kx) * channels
-                piece = part[kx * share : (kx + 1) * share]
-                if fresh[0]:
-                    sums[:, at : at + channels] = piece
-                else:
-                    sums[:, at : at + channels] += piece
-        fresh[0] = False
-
-    fresh = [True]
-    line_rows = 4 * rows
-    side = line_rows + line_rows // 2
-    forward_first(2)
-    forward_second(1)
-    wait_partner(0)
-    wait_partner(1)
-    stage(half * (height - side), side)
-    forward_first(3)
     forward_second(2)
     wait_partner(2)
     stage(side, height - 2 * side)
@@ -300,8 +321,15 @@
 
     for one, got in grad_copies:
         one.wait_send()
-    for one in x_copy + y_copy + dx_copy + dy_copy + z_copy + [gx, gp0, gp1]:
+    for one in x_copy + y_copy + dx_copy + dy_copy + [z_near, gx, gp0, gp1]:
         one.wait_send()
+
+    @pl.when(is_middle)
+    def _():
+        z_across.wait_send()
+        for n in z_pass:
+            z_pass[n].wait_send()
+
     for pair in p_copy:
         pair[0].wait_send()
         pair[1].wait_send()
@@ -334,7 +362,8 @@
             pltpu.VMEM((2 * lines, grad_share, channels), jnp.float32),
         ]
         + [dma((2,))]
-        + [dma((lines,))] * 10
+        + [dma((lines + 1,)), dma((lines,))]
+        + [dma((lines,))] * 8
         + [dma((lines, 2))] * 2
         + [dma((3,))] * 2
         + [dma((2 * lines,))] * 2,

time: 30.7 us -> 30.1 us (0.980)
  Pallas kernels: 26.6 us -> 26 us
    pallas_call x1, Pallas kernels: 26.6 us -> 26 us  [kernel_form(): pl.pallas_call(gather_kernel, out_shape=(jax.ShapeDtypeStruct((share, wid...]
where the time goes in v2:
time: 30.1 us; the launch traced here: 29.9 us
  Pallas kernels  26 us (86%)
  local copies, waits for them, and re-layouts  1.68 us (6%)
  other arithmetic  1.55 us (5%)
  between operations  0.66 us (2%)
    pallas_call x1, Pallas kernels, kernel_form(): pl.pallas_call(gather_kernel, out_shape=(jax.ShapeDtypeStruct((share, wid...  26 us
    unnamed x8, local copies, waits for them, and re-layouts  1.68 us
    add x1, other arithmetic, kernel_form(): 0.5 * old_input_factor.astype(jnp.float32) + 0.5 / positions * input_sum  0.94 us
    add x1, other arithmetic, kernel_form(): grad_factor = 0.5 * old_grad_factor + 0.5 / positions * grad_sum  0.61 us

profile of v2, /device:TPU:0, one launch (start us, length us, event | category | flops | bytes accessed | tf_op | source)
XLA Modules:
  0.0 29.9 jit_solution(5351297634815821037)
XLA Ops:
  0.6 0.0 copy-start
  0.6 0.8 %copy-done = bf16[2,1,64,256]{3,2,1,0:T(8,128)(2,1)S(1)} copy-done((bf16[2,1,64,256]{3,2,1,0:T(8,128)(2,1)S(1)}, bf16[2,1,64,256]{3,2,1,0:T(8,128)(2,1)}, u32[]{:S(2)}) %copy-start) | copy-done | bytes 65560
  1.5 0.0 copy-start.1
  1.5 0.8 %copy-done.1 = bf16[2,1,64,256]{3,2,1,0:T(8,128)(2,1)S(1)} copy-done((bf16[2,1,64,256]{3,2,1,0:T(8,128)(2,1)S(1)}, bf16[2,1,64,256]{3,2,1,0:T(8,128)(2,1)}, u32[]{:S(2)}) %copy-start.1) | copy-done | bytes 65560
  2.3 0.0 copy-start.2
  2.3 26.0 %shard_map.59 = (f32[72,2304]{1,0:T(8,128)S(1)}, f32[16,256]{1,0:T(8,128)S(1)}) custom-call(bf16[2,1,64,256]{3,2,1,0:T(8,128)(2,1)S(1)} %copy-done, bf16[2,1,64,256]{3,2,1,0:T(8,128)(2,1)S(1)} %copy-done.1), custom_call_target="tpu_custom_call" | custom-call | flops 1358954496 | bytes 663552 | tf_op jit(solution)/shard_map/pallas_call | solution.py:350
  28.4 0.0 copy-done.2
  28.4 0.0 copy-start.3
  28.4 0.9 %multiply_add_fusion = f32[72,2304]{1,0:T(8,128)} fusion(f32[72,2304]{1,0:T(8,128)S(1)} %get-tuple-element.4, bf16[72,2304]{1,0:T(8,128)(2,1)S(1)} %copy-done.2), kind=kLoop, calls=%fused_computation | loop fusion | flops 663552 | bytes 1658880 | tf_op jit(solution)/shard_map/add | solution.py:378
  29.3 0.0 copy-done.3
  29.3 0.6 %multiply_add_fusion.1 = f32[16,256]{1,0:T(8,128)} fusion(f32[16,256]{1,0:T(8,128)S(1)} %get-tuple-element.5, f32[16,256]{1,0:T(8,128)S(1)} %copy-done.3), kind=kLoop, calls=%fused_computation.1 | loop fusion | flops 12288 | bytes 49152 | tf_op jit(solution)/shard_map/add | solution.py:379
Async XLA Ops:
  0.6 0.8 %copy-start = (bf16[2,1,64,256]{3,2,1,0:T(8,128)(2,1)S(1)}, bf16[2,1,64,256]{3,2,1,0:T(8,128)(2,1)}, u32[]{:S(2)}) copy-start(bf16[2,1,64,256]{3,2,1,0:T(8,128)(2,1)} %act.1) | copy-start | bytes 196612
  1.5 0.8 %copy-start.1 = (bf16[2,1,64,256]{3,2,1,0:T(8,128)(2,1)S(1)}, bf16[2,1,64,256]{3,2,1,0:T(8,128)(2,1)}, u32[]{:S(2)}) copy-start(bf16[2,1,64,256]{3,2,1,0:T(8,128)(2,1)} %grad.1) | copy-start | bytes 196612
  2.3 26.1 %copy-start.2 = (bf16[72,2304]{1,0:T(8,128)(2,1)S(1)}, bf16[72,2304]{1,0:T(8,128)(2,1)}, u32[]{:S(2)}) copy-start(bf16[72,2304]{1,0:T(8,128)(2,1)} %param.6) | copy-start | bytes 995332
  28.4 1.0 %copy-start.3 = (f32[16,256]{1,0:T(8,128)S(1)}, f32[16,256]{1,0:T(8,128)}, u32[]{:S(2)}) copy-start(f32[16,256]{1,0:T(8,128)} %param.7) | copy-start | bytes 49156

commit v3 on v2

--- a/solution.py
+++ b/solution.py
@@ -184,8 +184,6 @@
     gx = copy(grad, gbuf.at[1], sg.at[0], rg.at[0], to_x)
     gp0 = copy(grad, gbuf.at[2], sg.at[1], rg.at[1], to_p)
     gp1 = copy(gbuf.at[1], gbuf.at[3], sg.at[2], rg.at[2], to_p)
-    gp0.start()
-    gx.start()
 
     def forward_first(n):
         x_copy[n].wait_recv()
@@ -214,14 +212,16 @@
         p_copy[n][1].wait_recv()
 
     keep.wait()
+    forward_line(1)
     forward_first(0)
-    forward_line(1)
+    gp0.start()
+    gx.start()
+    forward_line(2)
+    forward_line(3)
+    forward_first(1)
+    forward_second(0)
     gx.wait_recv()
     gp1.start()
-    forward_line(2)
-    forward_second(0)
-    forward_first(1)
-    forward_line(3)
 
     keep_grad.wait()
     gp0.wait_recv()
@@ -285,9 +285,6 @@
     side = line_rows + line_rows // 2
     forward_first(2)
     forward_second(1)
-    wait_partner(0)
-    wait_partner(1)
-    stage(half * (height - side), side)
     forward_first(3)
     grad_copies = []
     for n, line in enumerate(order):
@@ -303,9 +300,12 @@
             grad_copies.append((one, got))
 
     forward_second(2)
+    wait_partner(0)
+    wait_partner(1)
+    stage(half * (height - side), side)
+    forward_second(3)
     wait_partner(2)
     stage(side, height - 2 * side)
-    forward_second(3)
     wait_partner(3)
     stage((1 - half) * (height - side), side)
 

time: 30.1 us -> 29.6 us (0.983)
  Pallas kernels: 26 us -> 25.4 us
    pallas_call x1, Pallas kernels: 26 us -> 25.4 us  [kernel_form(): pl.pallas_call(gather_kernel, out_shape=(jax.ShapeDtypeStruct((share, wid...]
where the time goes in v3:
time: 29.6 us; the launch traced here: 29.3 us
  Pallas kernels  25.4 us (86%)
  local copies, waits for them, and re-layouts  1.68 us (6%)
  other arithmetic  1.55 us (5%)
  between operations  0.66 us (2%)
    pallas_call x1, Pallas kernels, kernel_form(): pl.pallas_call(gather_kernel, out_shape=(jax.ShapeDtypeStruct((share, wid...  25.4 us
    unnamed x8, local copies, waits for them, and re-layouts  1.68 us
    add x1, other arithmetic, kernel_form(): 0.5 * old_input_factor.astype(jnp.float32) + 0.5 / positions * input_sum  0.94 us
    add x1, other arithmetic, kernel_form(): grad_factor = 0.5 * old_grad_factor + 0.5 / positions * grad_sum  0.61 us

profile of v3, /device:TPU:0, one launch (start us, length us, event | category | flops | bytes accessed | tf_op | source)
XLA Modules:
  0.0 29.3 jit_solution(14714957537263326929)
XLA Ops:
  0.6 0.0 copy-start
  0.6 0.8 %copy-done = bf16[2,1,64,256]{3,2,1,0:T(8,128)(2,1)S(1)} copy-done((bf16[2,1,64,256]{3,2,1,0:T(8,128)(2,1)S(1)}, bf16[2,1,64,256]{3,2,1,0:T(8,128)(2,1)}, u32[]{:S(2)}) %copy-start) | copy-done | bytes 65560
  1.5 0.0 copy-start.1
  1.5 0.8 %copy-done.1 = bf16[2,1,64,256]{3,2,1,0:T(8,128)(2,1)S(1)} copy-done((bf16[2,1,64,256]{3,2,1,0:T(8,128)(2,1)S(1)}, bf16[2,1,64,256]{3,2,1,0:T(8,128)(2,1)}, u32[]{:S(2)}) %copy-start.1) | copy-done | bytes 65560
  2.3 0.0 copy-start.2
  2.3 25.4 %shard_map.59 = (f32[72,2304]{1,0:T(8,128)S(1)}, f32[16,256]{1,0:T(8,128)S(1)}) custom-call(bf16[2,1,64,256]{3,2,1,0:T(8,128)(2,1)S(1)} %copy-done, bf16[2,1,64,256]{3,2,1,0:T(8,128)(2,1)S(1)} %copy-done.1), custom_call_target="tpu_custom_call" | custom-call | flops 1358954496 | bytes 663552 | tf_op jit(solution)/shard_map/pallas_call | solution.py:350
  27.7 0.0 copy-done.2
  27.7 0.0 copy-start.3
  27.7 0.9 %multiply_add_fusion = f32[72,2304]{1,0:T(8,128)} fusion(f32[72,2304]{1,0:T(8,128)S(1)} %get-tuple-element.4, bf16[72,2304]{1,0:T(8,128)(2,1)S(1)} %copy-done.2), kind=kLoop, calls=%fused_computation | loop fusion | flops 663552 | bytes 1658880 | tf_op jit(solution)/shard_map/add | solution.py:378
  28.7 0.0 copy-done.3
  28.7 0.6 %multiply_add_fusion.1 = f32[16,256]{1,0:T(8,128)} fusion(f32[16,256]{1,0:T(8,128)S(1)} %get-tuple-element.5, f32[16,256]{1,0:T(8,128)S(1)} %copy-done.3), kind=kLoop, calls=%fused_computation.1 | loop fusion | flops 12288 | bytes 49152 | tf_op jit(solution)/shard_map/add | solution.py:379
Async XLA Ops:
  0.6 0.8 %copy-start = (bf16[2,1,64,256]{3,2,1,0:T(8,128)(2,1)S(1)}, bf16[2,1,64,256]{3,2,1,0:T(8,128)(2,1)}, u32[]{:S(2)}) copy-start(bf16[2,1,64,256]{3,2,1,0:T(8,128)(2,1)} %act.1) | copy-start | bytes 196612
  1.5 0.8 %copy-start.1 = (bf16[2,1,64,256]{3,2,1,0:T(8,128)(2,1)S(1)}, bf16[2,1,64,256]{3,2,1,0:T(8,128)(2,1)}, u32[]{:S(2)}) copy-start(bf16[2,1,64,256]{3,2,1,0:T(8,128)(2,1)} %grad.1) | copy-start | bytes 196612
  2.3 25.4 %copy-start.2 = (bf16[72,2304]{1,0:T(8,128)(2,1)S(1)}, bf16[72,2304]{1,0:T(8,128)(2,1)}, u32[]{:S(2)}) copy-start(bf16[72,2304]{1,0:T(8,128)(2,1)} %param.6) | copy-start | bytes 995332
  27.7 1.0 %copy-start.3 = (f32[16,256]{1,0:T(8,128)S(1)}, f32[16,256]{1,0:T(8,128)}, u32[]{:S(2)}) copy-start(f32[16,256]{1,0:T(8,128)} %param.7) | copy-start | bytes 49156
